TPU v7x, 128 devices: a whole 4x4x4 slice. The times are simulated.
128 devices in a mesh: ctx: 16 (over y, x_lo, core), pb: 8 (over z, x_hi).
Axes of the slice: x: 4 (x_hi: 2, x_lo: 2; x = x_hi * 2 + x_lo), y: 4, z: 4, core: 2. Of those that a mesh axis runs over, the one named last changes fastest.
Arguments:
- embed_prev: bfloat16 [4096, 2048], P('ctx'), may hold values from -16 to 16
- w_query: bfloat16 [2048, 2048], P(None, 'pb'), may hold values from -1 to 1
- w_key: bfloat16 [2048, 2048], P(None, 'pb'), may hold values from -1 to 1
- w_value: bfloat16 [2048, 2048], P(None, 'pb'), may hold values from -0.125 to 0.125
- w_out: bfloat16 [2048, 2048], P('pb'), may hold values from -1 to 1
- byte_ids: int32 [4096, 8], P(('ctx', 'pb')), may hold values from 0 to 255
- pad_embed: bfloat16 [512], replicated, may hold values from -3 to 3
- byte_table: bfloat16 [256, 512], replicated, may hold values from -5 to 5
- w_link: bfloat16 [256, 512], replicated, may hold values from -0.375 to 0.375
- w_local_qkv: bfloat16 [512, 1536], replicated, may hold values from -1 to 1
- w_local_out: bfloat16 [512, 512], replicated, may hold values from -0.25 to 0.25
- w_vocab: bfloat16 [512, 256], replicated, may hold values from -3 to 3
Outputs:
- grad_query: bfloat16 [2048, 2048], P('ctx', 'pb')
- grad_key: bfloat16 [2048, 2048], P('ctx', 'pb')
- grad_value: bfloat16 [2048, 2048], P('ctx', 'pb')
- grad_out: bfloat16 [2048, 2048], P('pb', 'ctx')
All inputs are finite; a program needn't handle non-finite values.
Results may differ from a plain program's by a relative error of at most 0.035.
Values may be sent and summed in bfloat16 or wider, within the bound.
A program may use at most 128 MiB of HBM per device.

v0:
```python
import jax
import jax.numpy as jnp
from jax import lax
from jax.sharding import PartitionSpec as P

HD = 128
LHD = 64


epsilon = 1e-06
masked_value = -1e30


def rounded(values):
    return lax.optimization_barrier(values.astype(jnp.bfloat16)).astype(jnp.float32)


def rms_round(values):
    return (values * lax.rsqrt(jnp.mean(values * values, axis=1, keepdims=True) + epsilon)).astype(
        jnp.bfloat16
    )


def local_loss(
    glob, byte_ids, pad_embed, byte_table, w_link, w_local_qkv, w_local_out, w_vocab, total_bytes
):
    patches, patch = byte_ids.shape
    count_rows = patches * patch
    width = w_link.shape[1]
    heads = width // LHD
    pieces = glob.reshape(count_rows, glob.shape[1] // patch)
    earlier = jnp.concatenate(
        [jnp.zeros((patches, 1), jnp.int32), byte_ids[:, :-1]], axis=1
    ).reshape(count_rows, 1)
    leading = (lax.broadcasted_iota(jnp.int32, (patches, patch), 1) == 0).reshape(count_rows, 1)
    symbols = lax.broadcasted_iota(jnp.int32, (1, byte_table.shape[0]), 1)
    table_hot = jnp.logical_and(earlier == symbols, jnp.logical_not(leading)).astype(jnp.bfloat16)
    embedded = jnp.dot(table_hot, byte_table, preferred_element_type=jnp.float32)
    hidden_state = embedded + jnp.where(leading, pad_embed.astype(jnp.float32)[None, :], 0.0)
    hidden_state = hidden_state + jnp.dot(pieces, w_link, preferred_element_type=jnp.float32)
    mixed = jnp.dot(rms_round(hidden_state), w_local_qkv, preferred_element_type=jnp.float32)
    mixed = rounded(mixed).reshape(patches, patch, 3, heads, LHD)
    queries = mixed[:, :, 0]
    keys = mixed[:, :, 1]
    values = mixed[:, :, 2]
    scores = jnp.einsum("rphd,rqhd->rhpq", queries, keys) * LHD ** (-0.5)
    causal = lax.broadcasted_iota(jnp.int32, (patch, patch), 0) >= lax.broadcasted_iota(
        jnp.int32, (patch, patch), 1
    )
    scores = jnp.where(causal, scores, masked_value)
    weights = rounded(jax.nn.softmax(scores, axis=-1))
    attended = (
        jnp.einsum("rhpq,rqhd->rphd", weights, values)
        .astype(jnp.bfloat16)
        .reshape(count_rows, width)
    )
    hidden_state = hidden_state + jnp.dot(attended, w_local_out, preferred_element_type=jnp.float32)
    logits = jnp.dot(rms_round(hidden_state), w_vocab, preferred_element_type=jnp.float32)
    highest = lax.stop_gradient(jnp.max(logits, axis=1, keepdims=True))
    log_norm = highest[:, 0] + jnp.log(jnp.sum(jnp.exp(logits - highest), axis=1))
    target_hot = byte_ids.reshape(count_rows, 1) == lax.broadcasted_iota(
        jnp.int32, (1, logits.shape[1]), 1
    )
    picked = jnp.sum(jnp.where(target_hot, logits, 0.0), axis=1)
    return jnp.sum(log_norm - picked) / total_bytes


def positions(first_row, length):
    index = first_row + lax.iota(jnp.int32, length)
    return index


def cut_points(length):
    return ((0, length // 2), (length // 2, length))


def forward_step(state, queries, query_pos, keys, values, key_pos, scale):
    running, totals, summed = state
    scores = jnp.einsum("qhd,khd->qhk", queries, keys, preferred_element_type=jnp.float32) * scale
    allowed = key_pos[None, None, :] <= query_pos[:, None, None]
    scores = jnp.where(allowed, scores, masked_value)
    highest = jnp.maximum(running, jnp.max(scores, axis=2))
    weights = jnp.where(allowed, jnp.exp(scores - highest[:, :, None]), 0.0)
    factor = jnp.exp(running - highest)
    totals = totals * factor + jnp.sum(weights, axis=2)
    summed = summed * factor[:, :, None] + jnp.einsum(
        "qhk,khd->qhd", weights.astype(jnp.bfloat16), values, preferred_element_type=jnp.float32
    )
    return (highest, totals, summed)


def forward_guarded(state, queries, query_pos, keys, values, key_pos, scale):
    skipped = jnp.min(key_pos) > jnp.max(query_pos)
    return lax.cond(
        skipped,
        lambda current: current,
        lambda current: forward_step(current, queries, query_pos, keys, values, key_pos, scale),
        state,
    )


def score_grads(queries, grads, log_total, row_dots, query_pos, keys, values, key_pos, scale):
    scores = jnp.einsum("qhd,khd->qhk", queries, keys, preferred_element_type=jnp.float32) * scale
    allowed = key_pos[None, None, :] <= query_pos[:, None, None]
    probs = jnp.where(allowed, jnp.exp(scores - log_total[:, :, None]), 0.0)
    prob_grads = jnp.einsum("qhd,khd->qhk", grads, values, preferred_element_type=jnp.float32)
    score_grad = (probs * (prob_grads - row_dots[:, :, None]) * scale).astype(jnp.bfloat16)
    return (probs, score_grad)


def all_guarded(queries, grads, log_total, row_dots, query_pos, keys, values, key_pos, scale):

    def compute(unused):
        probs, score_grad = score_grads(
            queries, grads, log_total, row_dots, query_pos, keys, values, key_pos, scale
        )
        query_add = jnp.einsum("qhk,khd->qhd", score_grad, keys, preferred_element_type=jnp.float32)
        key_add = jnp.einsum(
            "qhk,qhd->khd", score_grad, queries, preferred_element_type=jnp.float32
        )
        value_add = jnp.einsum(
            "qhk,qhd->khd", probs.astype(jnp.bfloat16), grads, preferred_element_type=jnp.float32
        )
        return (query_add, key_add, value_add)

    def skip(unused):
        query_zero = jnp.zeros(queries.shape, jnp.float32)
        key_zero = jnp.zeros(keys.shape, jnp.float32)
        return (query_zero, key_zero, key_zero)

    return lax.cond(jnp.min(key_pos) > jnp.max(query_pos), skip, compute, 0)


def per_device(
    embed_prev,
    w_query,
    w_key,
    w_value,
    w_out,
    byte_ids,
    pad_embed,
    byte_table,
    w_link,
    w_local_qkv,
    w_local_out,
    w_vocab,
):
    count = lax.axis_size("ctx")
    place = lax.axis_index("ctx")
    rows = embed_prev.shape[0]
    half = rows // 2
    width = w_query.shape[1]
    heads = width // HD
    scale = HD ** (-0.5)
    halves = ((0, half), (half, rows))
    normed = rms_round(embed_prev.astype(jnp.float32))
    query = jnp.dot(normed, w_query, preferred_element_type=jnp.float32).astype(jnp.bfloat16)
    key = jnp.dot(normed, w_key, preferred_element_type=jnp.float32).astype(jnp.bfloat16)
    value = jnp.dot(normed, w_value, preferred_element_type=jnp.float32).astype(jnp.bfloat16)
    query3 = query.reshape(rows, heads, HD)
    query_pos = positions(place * rows, rows)
    empty_state = (
        jnp.full((half, heads), masked_value, jnp.float32),
        jnp.zeros((half, heads), jnp.float32),
        jnp.zeros((half, heads, HD), jnp.float32),
    )
    state = (empty_state, empty_state)
    keys = lax.all_gather(key, "ctx", axis=0, tiled=True)
    values = lax.all_gather(value, "ctx", axis=0, tiled=True)
    length = keys.shape[0]
    key_pos = positions(jnp.int32(0), length)
    keys3 = keys.reshape(length, heads, HD)
    values3 = values.reshape(length, heads, HD)
    updated = []
    for (low_row, high_row), attend_part in zip(halves, state):
        for low_key, high_key in cut_points(length):
            attend_part = forward_guarded(
                attend_part,
                query3[low_row:high_row],
                query_pos[low_row:high_row],
                keys3[low_key:high_key],
                values3[low_key:high_key],
                key_pos[low_key:high_key],
                scale,
            )
        updated.append(attend_part)
    final = tuple(updated)
    attended = jnp.concatenate([part[2] / part[1][:, :, None] for part in final], axis=0)
    log_total = jnp.concatenate([part[0] + jnp.log(part[1]) for part in final], axis=0)
    attn_spread = attended.reshape(rows, width).astype(jnp.bfloat16)
    glob = lax.psum_scatter(
        jnp.dot(attn_spread, w_out, preferred_element_type=jnp.float32).astype(jnp.bfloat16),
        "pb",
        scatter_dimension=0,
        tiled=True,
    )
    total_bytes = rows * count * byte_ids.shape[1]
    loss_value, pullback = jax.vjp(
        lambda inner: local_loss(
            inner,
            byte_ids,
            pad_embed,
            byte_table,
            w_link,
            w_local_qkv,
            w_local_out,
            w_vocab,
            total_bytes,
        ),
        glob,
    )
    glob_grad = pullback(jnp.ones_like(loss_value))[0]
    grad_full = lax.all_gather(glob_grad, "pb", axis=0, tiled=True)
    attn_grad_plain = lax.dot_general(
        grad_full, w_out, (((1,), (1,)), ((), ())), preferred_element_type=jnp.float32
    ).astype(jnp.bfloat16)
    grads3 = attn_grad_plain.reshape(rows, heads, HD)
    row_dots = jnp.sum(
        attn_grad_plain.astype(jnp.float32).reshape(rows, heads, HD)
        * attn_spread.astype(jnp.float32).reshape(rows, heads, HD),
        axis=2,
    )
    zero_half = jnp.zeros((half, heads, HD), jnp.float32)
    zero_sums = jnp.zeros((rows * count, 2, heads, HD), jnp.float32)
    keys = lax.all_gather(key, "ctx", axis=0, tiled=True)
    values = lax.all_gather(value, "ctx", axis=0, tiled=True)
    length = keys.shape[0]
    key_pos = positions(jnp.int32(0), length)
    keys3 = keys.reshape(length, heads, HD)
    values3 = values.reshape(length, heads, HD)
    query_parts_now = (zero_half, zero_half)
    key_sums = zero_sums
    updated = []
    for (low_row, high_row), part in zip(halves, query_parts_now):
        for low_key, high_key in cut_points(length):
            query_add, key_add, value_add = all_guarded(
                query3[low_row:high_row],
                grads3[low_row:high_row],
                log_total[low_row:high_row],
                row_dots[low_row:high_row],
                query_pos[low_row:high_row],
                keys3[low_key:high_key],
                values3[low_key:high_key],
                key_pos[low_key:high_key],
                scale,
            )
            part = part + query_add
            earlier_sums = lax.dynamic_slice_in_dim(key_sums, low_key, high_key - low_key, 0)
            key_sums = lax.dynamic_update_slice_in_dim(
                key_sums, earlier_sums + jnp.stack([key_add, value_add], axis=1), low_key, 0
            )
        updated.append(part)
    query_parts, key_sums = (tuple(updated), key_sums)
    own_sums = lax.psum_scatter(
        key_sums.astype(jnp.bfloat16), "ctx", scatter_dimension=0, tiled=True
    ).astype(jnp.float32)
    key_grad = own_sums[:, 0]
    value_grad = own_sums[:, 1]
    query_grad = jnp.concatenate(list(query_parts), axis=0)
    combined = jnp.concatenate(
        [
            query_grad.reshape(rows, width).astype(jnp.bfloat16),
            key_grad.reshape(rows, width).astype(jnp.bfloat16),
            value_grad.reshape(rows, width).astype(jnp.bfloat16),
        ],
        axis=1,
    )
    contract = (((0,), (0,)), ((), ()))
    first_terms = lax.dot_general(normed, combined, contract, preferred_element_type=jnp.float32)
    second_terms = lax.dot_general(
        grad_full, attn_spread, contract, preferred_element_type=jnp.float32
    )
    sums = lax.psum_scatter(
        jnp.concatenate([first_terms, second_terms], axis=1).astype(jnp.bfloat16),
        "ctx",
        scatter_dimension=0,
        tiled=True,
    ).astype(jnp.float32)
    grad_query = sums[:, :width].astype(jnp.bfloat16)
    grad_key = sums[:, width : 2 * width].astype(jnp.bfloat16)
    grad_value = sums[:, 2 * width : 3 * width].astype(jnp.bfloat16)
    grad_out = jnp.transpose(sums[:, 3 * width :]).astype(jnp.bfloat16)
    return (grad_query, grad_key, grad_value, grad_out)


def solution(mesh):
    in_specs = (
        P("ctx", None),
        P(None, "pb"),
        P(None, "pb"),
        P(None, "pb"),
        P("pb", None),
        P(("ctx", "pb"), None),
        P(),
        P(),
        P(),
        P(),
        P(),
        P(),
    )
    out_specs = (P("ctx", "pb"), P("ctx", "pb"), P("ctx", "pb"), P("pb", "ctx"))
    return jax.shard_map(
        per_device, mesh=mesh, in_specs=in_specs, out_specs=out_specs, check_vma=False
    )
```

profile of v0, /device:TPU:0, one launch (start us, length us, event | category | flops | bytes accessed | tf_op | source)
XLA Modules:
  0.0 513.8 jit_solution(6480566504440347956)
XLA Ops:
  23.2 25.1 %all-gather.4.cloned.1.call-done = bf16[4096,256]{1,0:T(8,128)(2,1)} async-done(((bf16[256,256]{1,0:T(8,128)(2,1)}), bf16[4096,256]{1,0:T(8,128)(2,1)}) %all-gather.4.cloned.1.call-update) | async-done | bytes 2097168 | tf_op jit(solution)/shard_map/all_gather | solution.py:225
  54.2 29.8 %all-gather.6.cloned.1.call-done = bf16[4096,256]{1,0:T(8,128)(2,1)} async-done(((bf16[256,256]{1,0:T(8,128)(2,1)}), bf16[4096,256]{1,0:T(8,128)(2,1)}) %all-gather.6.cloned.1.call-update) | async-done | bytes 2097168 | tf_op jit(solution)/shard_map/all_gather | solution.py:169
  89.1 4.2 conditional.10
  94.0 4.2 conditional.8
  103.2 77.2 %reduce-scatter.6.cloned.1.call-done = bf16[32,2048]{1,0:T(8,128)(2,1)} async-done(((bf16[256,2048]{1,0:T(8,128)(2,1)}), bf16[32,2048]{1,0:T(8,128)(2,1)}) %reduce-scatter.6.cloned.1.call-update) | async-done | bytes 131088 | tf_op jit(solution)/shard_map/reduce_scatter | solution.py:191
  222.4 45.4 %all-gather.8.cloned.1.call-done = bf16[256,2048]{1,0:T(8,128)(2,1)} async-done(((bf16[32,2048]{1,0:T(8,128)(2,1)}), bf16[256,2048]{1,0:T(8,128)(2,1)}) %all-gather.8.cloned.1.call-update) | async-done | bytes 1048592 | tf_op jit(solution)/shard_map/all_gather | solution.py:213
  270.0 17.5 %conditional.12 = (f32[128,2,128]{0,2,1:T(8,128)S(1)}, f32[2048,1,2,128]{0,3,2,1:T(8,128)}, f32[2048,1,2,128]{0,3,2,1:T(8,128)}) conditional(s32[]{:T(128)} %convert_element_type.168, (s32[2048]{0:T(1024)S(1)}, s32[128]{0:T(128)S(1)}, bf16[2048,2,128]{2,1,0:T(2,128)(2,1)}, bf16[128,2,128]{0,2,1:T(8,128)(2,1)S(1)}, f32[128,2]{0,1:T(2,128)S(1)}, ...), branch_computations={%region_32.33_spmd, %region_33.34_spmd} | conditional | flops 675545088 | bytes 43133548 | solution.py:131
  275.3 3.0 convolution_bitcast_fusion.4
  278.3 2.9 copy.286
  281.3 3.4 convolution_bitcast_fusion.3
  284.6 2.9 copy.288
  287.5 3.2 constant_dynamic-update-slice_fusion.1
  290.7 3.2 conditional.13
  293.9 3.2 constant_dynamic-update-slice_fusion
  297.0 17.5 %conditional.14 = (f32[128,2,128]{0,2,1:T(8,128)S(1)}, f32[2048,1,2,128]{0,3,2,1:T(8,128)}, f32[2048,1,2,128]{0,3,2,1:T(8,128)}) conditional(s32[]{:T(128)} %convert_element_type.175, (s32[2048]{0:T(1024)S(1)}, s32[128]{0:T(128)S(1)}, bf16[2048,2,128]{2,1,0:T(2,128)(2,1)}, bf16[128,2,128]{0,2,1:T(8,128)(2,1)S(1)}, f32[128,2]{0,1:T(2,128)S(1)}, ...), branch_computations={%region_36.37_spmd, %region_37.38_spmd} | conditional | flops 675545088 | bytes 43133548 | solution.py:131
  302.2 3.1 convolution_bitcast_fusion.12
  305.3 2.9 copy.298
  308.2 3.4 convolution_bitcast_fusion.11
  311.6 2.9 copy.300
  314.5 3.5 conditional.15
  318.0 3.9 maximum_maximum_fusion
  331.9 93.3 %reduce-scatter.8.cloned.1.call-done = bf16[256,2,2,128]{0,3,2,1:T(8,128)(2,1)} async-done(((bf16[4096,2,2,128]{0,3,2,1:T(8,128)(2,1)}), bf16[256,2,2,128]{0,3,2,1:T(8,128)(2,1)}) %reduce-scatter.8.cloned.1.call-update) | async-done | bytes 262160 | tf_op jit(solution)/shard_map/reduce_scatter | solution.py:254
  429.7 6.4 %copy.278 = bf16[2048,1024]{1,0:T(8,128)(2,1)} copy(bf16[2048,1024]{0,1:T(8,128)(2,1)} %pad_maximum_fusion) | data formatting | bytes 8388608
  436.1 68.2 %reduce-scatter.10.cloned.1.call-done = bf16[128,1024]{1,0:T(8,128)(2,1)} async-done(((bf16[2048,1024]{1,0:T(8,128)(2,1)}), bf16[128,1024]{1,0:T(8,128)(2,1)}) %reduce-scatter.10.cloned.1.call-update) | async-done | bytes 262160
  (260 shorter events, 112.8 us)
Async XLA Ops:
  7.2 174.5 %copy-start = (bf16[512,1536]{1,0:T(8,128)(2,1)S(1)}, bf16[512,1536]{1,0:T(8,128)(2,1)}, u32[]{:S(2)}) copy-start(bf16[512,1536]{1,0:T(8,128)(2,1)} %param.37) | copy-start | bytes 4718596
  7.2 41.1 %all-gather.4.cloned.1.call-start = ((), (), s32[]{:S(2)}) async-start(), calls=%async_computation.3 | async-start | bytes 2228224 | tf_op jit(solution)/shard_map/all_gather | solution.py:225
  8.9 12.4 %copy-start.58 = (f32[256]{0:T(256)}, f32[256]{0:T(256)S(1)}, u32[]{:S(2)}) copy-start(f32[256]{0:T(256)S(1)} %add_rsqrt_fusion) | copy-start | bytes 3076
  11.6 72.3 %all-gather.6.cloned.1.call-start = ((), (), s32[]{:S(2)}) async-start(), calls=%async_computation.4 | async-start | bytes 2228224 | tf_op jit(solution)/shard_map/all_gather | solution.py:169
  14.1 166.2 %reduce-scatter.6.cloned.1.call-start = ((), (), s32[]{:S(2)}) async-start(), calls=%async_computation.5 | async-start | bytes 1179648 | tf_op jit(solution)/shard_map/reduce_scatter | solution.py:191
  15.4 77.9 %copy-start.47 = (s32[128]{0:T(128)}, s32[128]{0:T(128)S(1)}, u32[]{:S(2)}) copy-start(s32[128]{0:T(128)S(1)} %get-tuple-element.602) | copy-start | bytes 1540
  15.4 82.7 %copy-start.49 = (s32[128]{0:T(128)}, s32[128]{0:T(128)S(1)}, u32[]{:S(2)}) copy-start(s32[128]{0:T(128)S(1)} %get-tuple-element.601) | copy-start | bytes 1540
  23.2 70.1 %copy-start.37 = (bf16[128,256]{0,1:T(8,128)(2,1)}, bf16[128,256]{0,1:T(8,128)(2,1)S(1)}, u32[]{:S(2)}) copy-start(bf16[128,256]{0,1:T(8,128)(2,1)S(1)} %get-tuple-element.598) | copy-start | bytes 196612
  23.2 74.9 %copy-start.39 = (bf16[128,256]{0,1:T(8,128)(2,1)}, bf16[128,256]{0,1:T(8,128)(2,1)S(1)}, u32[]{:S(2)}) copy-start(bf16[128,256]{0,1:T(8,128)(2,1)S(1)} %get-tuple-element.597) | copy-start | bytes 196612
  89.1 9.1 %copy-start.3 = (bf16[2048,2,128]{2,1,0:T(2,128)(2,1)}, bf16[2048,2,128]{2,1,0:T(2,128)(2,1)S(1)}, u32[]{:S(2)}) copy-start(bf16[2048,2,128]{2,1,0:T(2,128)(2,1)S(1)} %slice.164) | copy-start | bytes 3145732
  98.9 82.4 %copy-start.34 = (bf16[256,512]{1,0:T(8,128)(2,1)S(1)}, bf16[256,512]{1,0:T(8,128)(2,1)}, u32[]{:S(2)}) copy-start(bf16[256,512]{1,0:T(8,128)(2,1)} %param.36) | copy-start | bytes 786436
  101.7 166.2 %all-gather.8.cloned.1.call-start = ((), (), s32[]{:S(2)}) async-start(), calls=%async_computation.6 | async-start | bytes 1179648 | tf_op jit(solution)/shard_map/all_gather | solution.py:213
  102.9 86.9 %copy-start.62 = (pred[8,8]{1,0:T(8,128)(4,1)}, pred[8,8]{1,0:T(8,128)(4,1)S(1)}, u32[]{:S(2)}) copy-start(pred[8,8]{1,0:T(8,128)(4,1)S(1)} %iota_compare_fusion.3) | copy-start | bytes 196
  185.6 8.3 %copy-start.25 = (bf16[32,8,1,8,64]{4,3,2,1,0:T(8,128)(2,1)}, bf16[32,8,1,8,64]{4,3,2,1,0:T(8,128)(2,1)S(1)}, u32[]{:S(2)}) copy-start(bf16[32,8,1,8,64]{4,3,2,1,0:T(8,128)(2,1)S(1)} %get-tuple-element.586) | copy-start | bytes 786436
  221.6 48.4 %copy-start.5 = (bf16[2048,2,128]{2,1,0:T(2,128)(2,1)S(1)}, bf16[2048,2,128]{2,1,0:T(2,128)(2,1)}, u32[]{:S(2)}) copy-start(bf16[2048,2,128]{2,1,0:T(2,128)(2,1)} %slice.162) | copy-start | bytes 3145732
  221.6 48.4 %copy-start.40 = (bf16[128,256]{0,1:T(8,128)(2,1)S(1)}, bf16[128,256]{0,1:T(8,128)(2,1)}, u32[]{:S(2)}) copy-start(bf16[128,256]{0,1:T(8,128)(2,1)} %copy-done.39) | copy-start | bytes 196612
  221.6 48.4 %copy-start.50 = (s32[128]{0:T(128)S(1)}, s32[128]{0:T(128)}, u32[]{:S(2)}) copy-start(s32[128]{0:T(128)} %copy-done.49) | copy-start | bytes 1540
  222.4 202.9 %reduce-scatter.8.cloned.1.call-start = ((), (), s32[]{:S(2)}) async-start(), calls=%async_computation.7 | async-start | bytes 4456448 | tf_op jit(solution)/shard_map/reduce_scatter | solution.py:254
  270.0 17.5 %copy-start.4 = (bf16[2048,2,128]{2,1,0:T(2,128)(2,1)S(1)}, bf16[2048,2,128]{2,1,0:T(2,128)(2,1)}, u32[]{:S(2)}) copy-start(bf16[2048,2,128]{2,1,0:T(2,128)(2,1)} %copy-done.3) | copy-start | bytes 3145732
  318.0 5.9 %copy-start.21 = (f32[2048,1,2,128]{0,3,2,1:T(8,128)S(1)}, f32[2048,1,2,128]{0,3,2,1:T(8,128)}, u32[]{:S(2)}) copy-start(f32[2048,1,2,128]{0,3,2,1:T(8,128)} %get-tuple-element.558) | copy-start | bytes 6291460
  330.0 96.2 %copy-start.32 = (bf16[256,2048]{1,0:T(8,128)(2,1)S(1)}, bf16[256,2048]{1,0:T(8,128)(2,1)}, u32[]{:S(2)}) copy-start(bf16[256,2048]{1,0:T(8,128)(2,1)} %param.28) | copy-start | bytes 3145732
  330.0 96.2 %copy-start.59 = (f32[256]{0:T(256)S(1)}, f32[256]{0:T(256)}, u32[]{:S(2)}) copy-start(f32[256]{0:T(256)} %copy-done.58) | copy-start | bytes 3076
  330.0 174.3 %reduce-scatter.10.cloned.1.call-start = ((), (), s32[]{:S(2)}) async-start(), calls=%async_computation.8 | async-start | bytes 4456448
  436.1 70.6 %copy-start.1 = (bf16[512,1536]{1,0:T(8,128)(2,1)S(1)}, bf16[512,1536]{1,0:T(8,128)(2,1)}, u32[]{:S(2)}) copy-start(bf16[512,1536]{1,0:T(8,128)(2,1)} %param.37) | copy-start | bytes 4718596
  (44 other events, 95.2 us)
Sparse Core Ops, SparseCore 0:
  11.8 36.4 all-gather.3
  50.0 33.9 all-gather.5
  101.8 78.4 reduce-scatter.5
  222.5 45.3 all-gather.7
  330.1 95.0 reduce-scatter.7
  436.2 68.0 reduce-scatter.9
where the time goes:
time: 524 us; the launch traced here: 514 us
  waiting for transfers between devices  339 us (65%)
  local copies, waits for them, and re-layouts  78.8 us (15%)
  matrix products  51.8 us (10%)
  other arithmetic  22.2 us (4%)
  between operations  20.4 us (4%)
    reduce_scatter x1, waiting for transfers between devices, per_device(): lax.psum_scatter(key_sums.astype(jnp.bfloat16), 'ctx', scatter_dimension=...  93.3 us
    reduce_scatter x1, waiting for transfers between devices, per_device(): lax.psum_scatter(jnp.dot(attn_spread, w_out, preferred_element_type=jnp.f...  77.2 us
    unnamed x7, waiting for transfers between devices  68.3 us
    all_gather x1, waiting for transfers between devices, per_device(): grad_full = lax.all_gather(glob_grad, 'pb', axis=0, tiled=True)  45.4 us
    all_gather x1, waiting for transfers between devices, per_device(): values = lax.all_gather(value, 'ctx', axis=0, tiled=True)  29.8 us
    all_gather x1, waiting for transfers between devices, per_device(): keys = lax.all_gather(key, 'ctx', axis=0, tiled=True)  25.1 us
    unnamed x113, local copies, waits for them, and re-layouts  16.7 us
    cond x6, local copies, waits for them, and re-layouts, all_guarded(): return lax.cond(jnp.min(key_pos) > jnp.max(query_pos), skip, compute, 0)  11.8 us
  transfers between devices with their start and end apart: 6, of which 6 were waited for; matrix products, arithmetic and copies ran while one was open for 3% of the time, Pallas kernels for 0%

commit v1 on v0

v1 whole, which is shorter than its diff:
```python
import functools

import jax
import jax.numpy as jnp
from jax import lax
from jax.experimental import pallas as pl
from jax.experimental.pallas import tpu as pltpu
from jax.sharding import PartitionSpec as P

HD = 128
LHD = 64
PATCH = 8
EPSILON = 1e-06
MASKED = -1e30
MESH = pl.DeviceIdType.MESH
BF = jnp.bfloat16
F32 = jnp.float32


def nn(left, right):
    return lax.dot_general(left, right, (((1,), (0,)), ((), ())), preferred_element_type=F32)


def nt(left, right):
    return lax.dot_general(left, right, (((1,), (1,)), ((), ())), preferred_element_type=F32)


def tn(left, right):
    return lax.dot_general(left, right, (((0,), (0,)), ((), ())), preferred_element_type=F32)


def loop(low, high, body):
    def step(index, unused):
        body(index)
        return unused

    lax.fori_loop(low, high, step, 0)


def row_form(column, rows):
    return jnp.transpose(jnp.broadcast_to(column, (rows, HD)))[0:8]


def rms_inverse(values):
    return lax.rsqrt(jnp.mean(values * values, axis=1, keepdims=True) + EPSILON)


def rms_back(values, inverse, grad):
    width = values.shape[1]
    dots = jnp.sum(grad * values, axis=1, keepdims=True)
    return inverse * grad - values * (inverse * inverse * inverse * dots * (1.0 / width))


def step_kernel(
    sizes,
    embed,
    w_query,
    w_key,
    w_value,
    w_out,
    ids,
    pad_embed,
    table,
    w_link,
    w_mix,
    w_local_out,
    w_vocab,
    grad_query,
    grad_key,
    grad_value,
    grad_out,
    normed,
    kv_send,
    kv_all,
    q_send,
    q_all,
    run_max,
    run_sum,
    run_out,
    att_head,
    att_pair,
    lse_col,
    lse_all,
    glob_part,
    glob_in,
    hidden,
    mixed,
    weights,
    d_mixed,
    grad_all,
    da_send,
    da_all,
    dots_send,
    dots_all,
    dq_acc,
    dk_acc,
    dv_acc,
    wq_send,
    wo_send,
    wkv_send,
    wq_in,
    wo_in,
    wkv_in,
    kv_s,
    kv_r,
    q_s,
    q_r,
    da_s,
    da_r,
    dots_s,
    dots_r,
    wq_s,
    wq_r,
    wo_s,
    wo_r,
    wkv_s,
    wkv_r,
    lse_s,
    lse_r,
    glob_s,
    glob_r,
    grad_s,
    grad_r,
    norm_s,
    norm_r,
    att_s,
    att_r,
    full_s,
    full_r,
):
    nctx, npb = sizes
    chips = nctx // 2
    rows, wide = embed.shape
    patches = rows // npb
    bytes_here = patches * PATCH
    scale = HD ** (-0.5)
    place = lax.axis_index("ctx")
    part = lax.axis_index("pb")
    chip = place // 2
    core = place % 2
    other = place + 1 - 2 * core

    def ctx_copy(src, dst, send, recv, peer):
        return pltpu.make_async_remote_copy(
            src_ref=src,
            dst_ref=dst,
            send_sem=send,
            recv_sem=recv,
            device_id=(peer, part),
            device_id_type=MESH,
        )

    def pb_copy(src, dst, send, recv, peer):
        return pltpu.make_async_remote_copy(
            src_ref=src,
            dst_ref=dst,
            send_sem=send,
            recv_sem=recv,
            device_id=(place, peer),
            device_id_type=MESH,
        )

    def each_peer(wanted, action):
        def one(step):
            peer = (place + step) % nctx

            @pl.when(wanted(peer // 2))
            def _():
                action(peer)

        loop(1, nctx, one)

    def each_part(action):
        loop(1, npb, lambda step: action((part + step) % npb))

    later = lambda at: at >= chip
    earlier = lambda at: at <= chip
    anyone = lambda at: at >= 0

    barrier = pltpu.get_barrier_semaphore()

    def greet_ctx(peer):
        pl.semaphore_signal(barrier, inc=1, device_id=(peer, part), device_id_type=MESH)

    def greet_part(peer):
        pl.semaphore_signal(barrier, inc=1, device_id=(place, peer), device_id_type=MESH)

    each_peer(anyone, greet_ctx)
    each_part(greet_part)

    tile_rows = min(32, rows)

    def norm_rows(step):
        here = pl.ds(pl.multiple_of(step * tile_rows, tile_rows), tile_rows)
        values = embed[here, :].astype(F32)
        normed[core, here, :] = (values * rms_inverse(values)).astype(BF)

    loop(0, rows // tile_rows, norm_rows)
    own_normed = normed[core]
    for slot, weight in ((0, w_key), (1, w_value)):
        product = nn(own_normed, weight[...]).astype(BF)
        kv_send[0, slot] = product[:, :HD]
        kv_send[1, slot] = product[:, HD:]
    pl.semaphore_wait(barrier, nctx + npb - 2)

    def kv_copy(peer):
        return ctx_copy(
            kv_send.at[peer % 2], kv_all.at[:, place], kv_s.at[peer], kv_r.at[place], peer
        )

    each_peer(later, lambda peer: kv_copy(peer).start())
    kv_all[:, place] = kv_send[core]
    product = nn(own_normed, w_query[...]).astype(BF)
    q_send[0] = product[:, :HD]
    q_send[1] = product[:, HD:]

    def q_copy(peer):
        return ctx_copy(q_send.at[peer % 2], q_all.at[place], q_s.at[peer], q_r.at[place], peer)

    q_copy(other).start()
    q_all[place] = q_send[core]

    def norm_copy(index):
        return ctx_copy(normed.at[index], normed.at[index], norm_s, norm_r, other)

    norm_copy(core).start()
    strictly_earlier = lambda at: at < chip
    each_peer(strictly_earlier, lambda peer: q_copy(peer).start())

    def kv_wait(peer):
        ctx_copy(kv_send.at[0], kv_all.at[:, peer], kv_s.at[peer], kv_r.at[peer], peer).wait_recv()

    def q_wait(peer):
        ctx_copy(q_send.at[0], q_all.at[peer], q_s.at[peer], q_r.at[peer], peer).wait_recv()

    first = 2 * chip
    pair_rows = 2 * rows

    def keys_of(at):
        return kv_all[0, pl.ds(2 * at, 2)].reshape(pair_rows, HD)

    def values_of(at):
        return kv_all[1, pl.ds(2 * at, 2)].reshape(pair_rows, HD)

    def diagonal(half, keys_down):
        shape = (rows, pair_rows)
        here = lax.broadcasted_iota(jnp.int32, shape, 0) + half * rows
        there = lax.broadcasted_iota(jnp.int32, shape, 1)
        return (there >= here) if keys_down else (there <= here)

    run_max[...] = jnp.full(run_max.shape, MASKED, F32)
    run_sum[...] = jnp.zeros(run_sum.shape, F32)
    run_out[...] = jnp.zeros(run_out.shape, F32)

    def attend(half, at, on_diagonal):
        scores = nt(q_all[first + half], keys_of(at)) * scale
        if on_diagonal:
            scores = jnp.where(diagonal(half, False), scores, MASKED)
        before = run_max[half, :, 0:1]
        highest = jnp.maximum(before, jnp.max(scores, axis=1, keepdims=True))
        exps = jnp.exp(scores - highest)
        factor = jnp.exp(before - highest)
        total = run_sum[half, :, 0:1] * factor + jnp.sum(exps, axis=1, keepdims=True)
        run_out[half] = run_out[half] * factor + nn(exps.astype(BF), values_of(at))
        run_max[half] = jnp.broadcast_to(highest, (rows, HD))
        run_sum[half] = jnp.broadcast_to(total, (rows, HD))

    kv_wait(other)
    q_wait(other)
    for half in (0, 1):
        attend(half, chip, True)

    def attend_earlier(step):
        at = chip - step
        kv_wait(2 * at)
        kv_wait(2 * at + 1)
        for half in (0, 1):
            attend(half, at, False)

    loop(1, chip + 1, attend_earlier)
    for half in (0, 1):
        att_head[half] = (run_out[half] / run_sum[half]).astype(BF)
        log_total = run_max[half] + jnp.log(run_sum[half])
        lse_col[half] = log_total
        lse_all[chip, half] = jnp.transpose(log_total)[0:8]

    def att_copy():
        return ctx_copy(att_head.at[1 - core], att_pair.at[core], att_s, att_r, other)

    att_copy().start()
    att_pair[core] = att_head[core]

    def lse_copy(at):
        return ctx_copy(
            lse_all.at[chip], lse_all.at[chip], lse_s.at[at], lse_r.at[chip], 2 * at + core
        )

    loop(0, chip, lambda at: lse_copy(at).start())
    ctx_copy(att_head.at[0], att_pair.at[1 - core], att_s, att_r, other).wait_recv()

    both_heads = jnp.concatenate([att_pair[0], att_pair[1]], axis=1)
    out_tile = min(512, wide)

    def out_columns(step):
        here = pl.ds(pl.multiple_of(step * out_tile, out_tile), out_tile)
        product = nn(both_heads, w_out[:, here]).astype(BF)
        glob_part[:, :, here] = product.reshape(npb, patches, out_tile)

    loop(0, wide // out_tile, out_columns)

    def glob_copy(peer):
        return pb_copy(
            glob_part.at[peer], glob_in.at[part], glob_s.at[peer], glob_r.at[part], peer
        )

    each_part(lambda peer: glob_copy(peer).start())
    glob_in[part] = glob_part[part]

    ids_here = ids[...]
    targets = jnp.concatenate([ids_here[:, b : b + 1] for b in range(PATCH)], axis=0)
    nothing = jnp.full((patches, 1), -1, jnp.int32)
    preceding = jnp.concatenate(
        [nothing] + [ids_here[:, b : b + 1] for b in range(PATCH - 1)], axis=0
    )
    symbols = lax.broadcasted_iota(jnp.int32, (bytes_here, table.shape[0]), 1)
    table_hot = (preceding == symbols).astype(BF)
    leading = preceding < 0
    hidden[...] = nn(table_hot, table[...]) + jnp.where(
        leading, pad_embed[...].astype(F32), 0.0
    )

    def glob_wait(peer):
        pb_copy(
            glob_part.at[0], glob_in.at[peer], glob_s.at[peer], glob_r.at[peer], peer
        ).wait_recv()

    each_part(glob_wait)
    glob = glob_in[0].astype(F32)
    for index in range(1, npb):
        glob = glob + glob_in[index].astype(F32)
    glob = glob.astype(BF)
    byte_wide = wide // PATCH
    pieces = jnp.concatenate(
        [glob[:, b * byte_wide : (b + 1) * byte_wide] for b in range(PATCH)], axis=0
    )
    hidden[...] += nn(pieces, w_link[...])
    hidden_one = hidden[...]
    inverse_one = rms_inverse(hidden_one)
    mixed[...] = nn((hidden_one * inverse_one).astype(BF), w_mix[...]).astype(BF)
    local_wide = w_link.shape[1]
    row_index = lax.broadcasted_iota(jnp.int32, (bytes_here, bytes_here), 0)
    column_index = lax.broadcasted_iota(jnp.int32, (bytes_here, bytes_here), 1)
    same = jnp.logical_and(
        lax.rem(row_index, patches) == lax.rem(column_index, patches), column_index <= row_index
    )
    lane = lax.broadcasted_iota(jnp.int32, (bytes_here, 2 * LHD), 1)
    halves = (lane < LHD, lane >= LHD)
    pairs = local_wide // (2 * LHD)

    def pair_of(block, pair):
        low = block * local_wide + pair * 2 * LHD
        return mixed[:, low : low + 2 * LHD]

    def kept(values, side):
        return jnp.where(halves[side], values, jnp.zeros_like(values))

    local_att = []
    for pair in range(pairs):
        summed = None
        for side in (0, 1):
            scores = nt(kept(pair_of(0, pair), side), pair_of(1, pair)) * LHD ** (-0.5)
            scores = jnp.where(same, scores, MASKED)
            exps = jnp.exp(scores - jnp.max(scores, axis=1, keepdims=True))
            soft = exps / jnp.sum(exps, axis=1, keepdims=True)
            weights[2 * pair + side] = soft
            term = nn(soft.astype(BF), kept(pair_of(2, pair), side))
            summed = term if summed is None else summed + term
        local_att.append(summed.astype(BF))
    hidden_two = hidden[...] + nn(jnp.concatenate(local_att, axis=1), w_local_out[...])
    inverse_two = rms_inverse(hidden_two)
    logits = nn((hidden_two * inverse_two).astype(BF), w_vocab[...])
    exps = jnp.exp(logits - jnp.max(logits, axis=1, keepdims=True))
    soft = exps / jnp.sum(exps, axis=1, keepdims=True)
    d_logits = (soft - jnp.where(targets == symbols, 1.0, 0.0)) * (
        1.0 / (rows * nctx * PATCH)
    )
    d_normed_two = nt(d_logits.astype(BF), w_vocab[...]).astype(BF).astype(F32)
    d_hidden = rms_back(hidden_two, inverse_two, d_normed_two)
    d_local_att = nt(d_hidden.astype(BF), w_local_out[...]).astype(BF)
    for pair in range(pairs):
        low = pair * 2 * LHD
        d_att = d_local_att[:, low : low + 2 * LHD]
        d_query = d_key = d_value = None
        for side in (0, 1):
            soft = weights[2 * pair + side]
            d_side = kept(d_att, side)
            d_soft = nt(d_side, pair_of(2, pair)).astype(BF).astype(F32)
            dots = jnp.sum(d_soft * soft, axis=1, keepdims=True)
            d_scores = (soft * (d_soft - dots) * LHD ** (-0.5)).astype(BF)
            value_term = tn(soft.astype(BF), d_side)
            query_term = nn(d_scores, kept(pair_of(1, pair), side))
            key_term = tn(d_scores, kept(pair_of(0, pair), side))
            if side == 0:
                d_query, d_key, d_value = query_term, key_term, value_term
            else:
                d_query, d_key, d_value = (
                    d_query + query_term,
                    d_key + key_term,
                    d_value + value_term,
                )
        for block, term in enumerate((d_query, d_key, d_value)):
            at = block * local_wide + low
            d_mixed[:, at : at + 2 * LHD] = term.astype(BF)
    d_normed_one = nt(d_mixed[...], w_mix[...]).astype(BF).astype(F32)
    d_hidden = d_hidden + rms_back(hidden[...], rms_inverse(hidden[...]), d_normed_one)
    d_pieces = nt(d_hidden.astype(BF), w_link[...]).astype(BF)
    for b in range(PATCH):
        grad_all[core, part, :, b * byte_wide : (b + 1) * byte_wide] = d_pieces[
            b * patches : (b + 1) * patches
        ]

    def grad_copy(peer):
        mine = grad_all.at[core, part]
        return pb_copy(mine, mine, grad_s.at[peer], grad_r.at[part], peer)

    def grad_wait(peer):
        theirs = grad_all.at[core, peer]
        pb_copy(theirs, theirs, grad_s.at[peer], grad_r.at[peer], peer).wait_recv()

    each_part(lambda peer: grad_copy(peer).start())
    each_part(grad_wait)

    def full_copy(index):
        return ctx_copy(grad_all.at[index], grad_all.at[index], full_s, full_r, other)

    full_copy(core).start()
    product = nt(grad_all[core].reshape(rows, wide), w_out[...]).astype(BF)
    for head in (0, 1):
        d_att = product[:, head * HD : (head + 1) * HD]
        da_send[head] = d_att
        dots = jnp.sum(d_att.astype(F32) * att_pair[head].astype(F32), axis=1, keepdims=True)
        dots_send[head] = row_form(dots, rows)

    def da_copy(peer):
        return ctx_copy(
            da_send.at[peer % 2], da_all.at[place], da_s.at[peer], da_r.at[place], peer
        )

    def dots_copy(peer):
        return ctx_copy(
            dots_send.at[peer % 2], dots_all.at[place], dots_s.at[peer], dots_r.at[place], peer
        )

    def da_start(peer):
        da_copy(peer).start()
        dots_copy(peer).start()

    def da_wait(peer):
        ctx_copy(da_send.at[0], da_all.at[peer], da_s.at[peer], da_r.at[peer], peer).wait_recv()
        ctx_copy(
            dots_send.at[0], dots_all.at[peer], dots_s.at[peer], dots_r.at[peer], peer
        ).wait_recv()

    each_peer(earlier, da_start)
    da_all[place] = da_send[core]
    dots_all[place] = dots_send[core]
    da_wait(other)

    dq_acc[...] = jnp.zeros(dq_acc.shape, F32)

    def query_back(half, at, on_diagonal):
        scores = nt(q_all[first + half], keys_of(at)) * scale
        probs = jnp.exp(scores - lse_col[half, :, 0:1])
        if on_diagonal:
            probs = jnp.where(diagonal(half, False), probs, 0.0)
        d_probs = nt(da_all[first + half], values_of(at))
        d_scores = (probs * (d_probs - run_sum[half, :, 0:1]) * scale).astype(BF)
        dq_acc[half] += nn(d_scores, keys_of(at))

    for half in (0, 1):
        dots = jnp.sum(
            da_all[first + half].astype(F32) * att_head[half].astype(F32), axis=1, keepdims=True
        )
        run_sum[half] = jnp.broadcast_to(dots, (rows, HD))
    for half in (0, 1):
        query_back(half, chip, True)

    def query_earlier(step):
        for half in (0, 1):
            query_back(half, chip - step, False)

    loop(1, chip + 1, query_earlier)

    block_wide = wide // nctx

    def turned(values):
        return jnp.transpose(values.reshape(pair_rows, HD).astype(F32)).astype(BF)

    def normed_block(owner):
        here = pl.ds(pl.multiple_of(owner * block_wide, block_wide), block_wide)
        return normed[:, :, here].reshape(pair_rows, block_wide)

    def wq_copy(peer):
        return ctx_copy(wq_send.at[peer], wq_in.at[place], wq_s.at[peer], wq_r.at[place], peer)

    def wo_copy(peer):
        return ctx_copy(wo_send.at[peer], wo_in.at[place], wo_s.at[peer], wo_r.at[place], peer)

    def wkv_copy(peer):
        return ctx_copy(wkv_send.at[peer], wkv_in.at[place], wkv_s.at[peer], wkv_r.at[place], peer)

    norm_copy(1 - core).wait_recv()
    dq_turned = turned(dq_acc[...].astype(BF))

    def wq_block(owner):
        wq_send[owner] = nn(dq_turned, normed_block(owner)).astype(BF)

    loop(0, nctx, wq_block)
    each_peer(anyone, lambda peer: wq_copy(peer).start())
    wq_in[place] = wq_send[place]

    full_copy(1 - core).wait_recv()
    att_turned = turned(att_head[...])

    def wo_block(owner):
        here = pl.ds(pl.multiple_of(owner * block_wide, block_wide), block_wide)
        wo_send[owner] = nn(
            att_turned, grad_all[:, :, :, here].reshape(pair_rows, block_wide)
        ).astype(BF)

    loop(0, nctx, wo_block)
    each_peer(anyone, lambda peer: wo_copy(peer).start())
    wo_in[place] = wo_send[place]

    dk_acc[...] = jnp.zeros(dk_acc.shape, F32)
    dv_acc[...] = jnp.zeros(dv_acc.shape, F32)

    def key_back(half, at, on_diagonal):
        queries = q_all[pl.ds(2 * at, 2)].reshape(pair_rows, HD)
        grads = da_all[pl.ds(2 * at, 2)].reshape(pair_rows, HD)
        log_total = jnp.concatenate([lse_all[at, 0, 0:1, :], lse_all[at, 1, 0:1, :]], axis=1)
        dots = jnp.concatenate([dots_all[2 * at, 0:1, :], dots_all[2 * at + 1, 0:1, :]], axis=1)
        scores = nt(kv_all[0, first + half], queries) * scale
        probs = jnp.exp(scores - log_total)
        if on_diagonal:
            probs = jnp.where(diagonal(half, True), probs, 0.0)
        d_probs = nt(kv_all[1, first + half], grads)
        d_scores = (probs * (d_probs - dots) * scale).astype(BF)
        dv_acc[half] += nn(probs.astype(BF), grads)
        dk_acc[half] += nn(d_scores, queries)

    for half in (0, 1):
        key_back(half, chip, True)

    def key_later(at):
        for peer in (2 * at, 2 * at + 1):
            q_wait(peer)
            da_wait(peer)
        ctx_copy(
            lse_all.at[at], lse_all.at[at], lse_s.at[at], lse_r.at[at], 2 * at + core
        ).wait_recv()
        for half in (0, 1):
            key_back(half, at, False)

    loop(chip + 1, chips, key_later)
    dk_turned = turned(dk_acc[...].astype(BF))
    dv_turned = turned(dv_acc[...].astype(BF))

    def wkv_block(owner):
        block = normed_block(owner)
        wkv_send[owner, 0] = nn(dk_turned, block).astype(BF)
        wkv_send[owner, 1] = nn(dv_turned, block).astype(BF)

    loop(0, nctx, wkv_block)
    each_peer(anyone, lambda peer: wkv_copy(peer).start())
    wkv_in[place] = wkv_send[place]

    def total_of(pick, head):
        total = pick(head).astype(F32)
        for index in range(1, chips):
            total = total + pick(2 * index + head).astype(F32)
        return total

    def wq_wait(peer):
        ctx_copy(wq_send.at[0], wq_in.at[peer], wq_s.at[peer], wq_r.at[peer], peer).wait_recv()

    def wo_wait(peer):
        ctx_copy(wo_send.at[0], wo_in.at[peer], wo_s.at[peer], wo_r.at[peer], peer).wait_recv()

    def wkv_wait(peer):
        ctx_copy(wkv_send.at[0], wkv_in.at[peer], wkv_s.at[peer], wkv_r.at[peer], peer).wait_recv()

    each_peer(anyone, wq_wait)
    for head in (0, 1):
        total = total_of(lambda index: wq_in[index], head)
        grad_query[:, head * HD : (head + 1) * HD] = jnp.transpose(total).astype(BF)
    each_peer(anyone, wo_wait)
    for head in (0, 1):
        total = total_of(lambda index: wo_in[index], head)
        grad_out[head * HD : (head + 1) * HD, :] = total.astype(BF)
    each_peer(anyone, wkv_wait)
    for head in (0, 1):
        total = total_of(lambda index: wkv_in[index, 0], head)
        grad_key[:, head * HD : (head + 1) * HD] = jnp.transpose(total).astype(BF)
        total = total_of(lambda index: wkv_in[index, 1], head)
        grad_value[:, head * HD : (head + 1) * HD] = jnp.transpose(total).astype(BF)

    each_peer(later, lambda peer: kv_copy(peer).wait_send())

    def sent_earlier(peer):
        q_copy(peer).wait_send()
        da_copy(peer).wait_send()
        dots_copy(peer).wait_send()

    each_peer(earlier, sent_earlier)
    loop(0, chip, lambda at: lse_copy(at).wait_send())
    norm_copy(core).wait_send()
    att_copy().wait_send()
    full_copy(core).wait_send()

    def sent_part(peer):
        glob_copy(peer).wait_send()
        grad_copy(peer).wait_send()

    each_part(sent_part)

    def sent_all(peer):
        wq_copy(peer).wait_send()
        wo_copy(peer).wait_send()
        wkv_copy(peer).wait_send()

    each_peer(anyone, sent_all)


def per_device(nctx, npb, *args):
    embed, w_query, w_key, w_value, w_out, ids, pad_embed, table, w_link, w_mix, w_lo, w_vocab = args
    rows, wide = embed.shape
    patches = rows // npb
    local_rows = patches * PATCH
    local_wide = w_link.shape[1]
    chips = nctx // 2
    block = wide // nctx
    vmem = pltpu.VMEM
    dma = pltpu.SemaphoreType.DMA
    scratch = [
        vmem((2, rows, wide), BF),
        vmem((2, 2, rows, HD), BF),
        vmem((2, nctx, rows, HD), BF),
        vmem((2, rows, HD), BF),
        vmem((nctx, rows, HD), BF),
        vmem((2, rows, HD), F32),
        vmem((2, rows, HD), F32),
        vmem((2, rows, HD), F32),
        vmem((2, rows, HD), BF),
        vmem((2, rows, HD), BF),
        vmem((2, rows, HD), F32),
        vmem((chips, 2, 8, rows), F32),
        vmem((npb, patches, wide), BF),
        vmem((npb, patches, wide), BF),
        vmem((local_rows, local_wide), F32),
        vmem((local_rows, 3 * local_wide), BF),
        vmem((local_wide // LHD, local_rows, local_rows), F32),
        vmem((local_rows, 3 * local_wide), BF),
        vmem((2, npb, patches, wide), BF),
        vmem((2, rows, HD), BF),
        vmem((nctx, rows, HD), BF),
        vmem((2, 8, rows), F32),
        vmem((nctx, 8, rows), F32),
        vmem((2, rows, HD), F32),
        vmem((2, rows, HD), F32),
        vmem((2, rows, HD), F32),
        vmem((nctx, HD, block), BF),
        vmem((nctx, HD, block), BF),
        vmem((nctx, 2, HD, block), BF),
        vmem((nctx, HD, block), BF),
        vmem((nctx, HD, block), BF),
        vmem((nctx, 2, HD, block), BF),
    ]
    scratch += [dma((nctx,))] * 14
    scratch += [dma((chips,))] * 2
    scratch += [dma((npb,))] * 4
    scratch += [dma] * 6
    whole = pl.BlockSpec(memory_space=pltpu.VMEM)
    tall = jax.ShapeDtypeStruct((block, 2 * HD), BF)
    return pl.pallas_call(
        functools.partial(step_kernel, (nctx, npb)),
        out_shape=(tall, tall, tall, jax.ShapeDtypeStruct((2 * HD, block), BF)),
        in_specs=[whole] * 12,
        out_specs=(whole,) * 4,
        scratch_shapes=scratch,
        compiler_params=pltpu.CompilerParams(
            collective_id=0, has_side_effects=True, vmem_limit_bytes=56 * 1024 * 1024
        ),
        name="step",
    )(
        embed, w_query, w_key, w_value, w_out, ids, pad_embed[None, :], table, w_link, w_mix,
        w_lo, w_vocab,
    )


def solution(mesh):
    in_specs = (
        P("ctx", None),
        P(None, "pb"),
        P(None, "pb"),
        P(None, "pb"),
        P("pb", None),
        P(("ctx", "pb"), None),
        P(),
        P(),
        P(),
        P(),
        P(),
        P(),
    )
    out_specs = (P("ctx", "pb"), P("ctx", "pb"), P("ctx", "pb"), P("pb", "ctx"))
    return jax.shard_map(
        functools.partial(per_device, mesh.shape["ctx"], mesh.shape["pb"]),
        mesh=mesh,
        in_specs=in_specs,
        out_specs=out_specs,
        check_vma=False,
    )
```

time: 524 us -> 123 us (0.23)
  the two profiles are of different devices: /device:TPU:0 before, /device:TPU:9 now
where the time goes in v1:
time: 123 us; the launch traced here: 121 us
  Pallas kernels  112 us (91%)
  local copies, waits for them, and re-layouts  8.52 us (7%)
    pallas_call x1, Pallas kernels, per_device(): pl.pallas_call(functools.partial(step_kernel, (nctx, npb)), out_shape=(ta...  112 us
    unnamed x5, local copies, waits for them, and re-layouts  7.26 us

profile of v1, /device:TPU:9, one launch (start us, length us, event | category | flops | bytes accessed | tf_op | source)
XLA Modules:
  0.0 120.8 jit_solution(5155302764572056236)
XLA Ops:
  0.6 1.3 %broadcast_in_dim.3.pad_embed = bf16[1,512]{1,0:T(2,128)(2,1)} reshape(bf16[512]{0:T(512)(128)(2,1)} %param.18) | data formatting | bytes 2048 | tf_op jit(solution)/shard_map/broadcast_in_dim | solution.py:696
  1.9 1.4 %copy.16.ids = s32[32,8]{1,0:T(8,128)} copy(s32[32,8]{0,1:T(8,128)} %param.17) | data formatting | bytes 2048 | tf_op args[5]
  3.3 111.6 %step.1 = (bf16[128,256]{1,0:T(8,128)(2,1)}, bf16[128,256]{1,0:T(8,128)(2,1)}, bf16[128,256]{1,0:T(8,128)(2,1)}, bf16[256,128]{1,0:T(8,128)(2,1)}) custom-call(bf16[256,2048]{1,0:T(8,128)(2,1)} %embed.1, bf16[2048,256]{1,0:T(8,128)(2,1)} %w_query.1, bf16[2048,256]{1,0:T(8,128)(2,1)} %w_key.1, bf16[2048,256]{1,0:T(8,128)(2,1)} %w_value.1, ...), custom_call_target="tpu_custom_call" | custom-call | tf_op jit(solution)/shard_map/step/pallas_call | solution.py:685
  114.9 1.5 %copy.21 = bf16[128,256]{1,0:T(8,128)(2,1)} copy(bf16[128,256]{1,0:T(8,128)(2,1)} %get-tuple-element.8) | data formatting | bytes 131072
  116.3 1.5 %copy.22 = bf16[128,256]{1,0:T(8,128)(2,1)} copy(bf16[128,256]{1,0:T(8,128)(2,1)} %get-tuple-element.9) | data formatting | bytes 131072
  117.8 1.5 %copy.23 = bf16[128,256]{1,0:T(8,128)(2,1)} copy(bf16[128,256]{1,0:T(8,128)(2,1)} %get-tuple-element.10) | data formatting | bytes 131072
  119.3 1.5 %copy.24 = bf16[256,128]{1,0:T(8,128)(2,1)} copy(bf16[256,128]{1,0:T(8,128)(2,1)} %get-tuple-element.11) | data formatting | bytes 131072
